TPU v7x, 512 devices: a whole 4x4x16 slice. The times are simulated.
512 devices in a mesh: dp: 32 (over z, core), tensor: 16 (over x, y).
Axes of the slice: x: 4, y: 4, z: 16, core: 2. Of those that a mesh axis runs over, the one named last changes fastest.
Arguments:
- activations: bfloat16 [16384, 8192], P('dp', 'tensor'), may hold values from -6 to 6
- kv_weight: bfloat16 [8192, 2048], P('tensor'), may hold values from -0.09375 to 0.09375
- pool_shrink: bfloat16 [128, 64, 8192], P('dp', None, 'tensor'), may hold values from -0.0625 to 0.0625
- pool_expand: bfloat16 [128, 64, 2048], P('dp', None, 'tensor'), may hold values from -0.75 to 0.75
- request_slot: int32 [16384], P('dp'), may hold values from 0 to 31
- slot_owner: int32 [1024, 1], P('dp'), may hold values from 0 to 31; in each aligned block of 32 rows (0 to 31, 32 to 63, ...) at most 2 rows name the same one
- slot_local: int32 [1024, 1], P('dp'), may hold values from 0 to 3
Outputs:
- projected: bfloat16 [16384, 2048], P('dp', 'tensor')
Inputs may be any that keep to these rules, and one draw needn't show every extreme that they name: `slot_owner`: among the 32 slots of one group (an aligned block of 32 rows) no owner appears more than 2 times, and some owner appears exactly 2 times in some group.
All inputs are finite; a program needn't handle non-finite values.
Results may differ from a plain program's by a relative error of at most 0.0037.
Values may be sent and summed in bfloat16 or wider, within the bound.
A program may use at most 64 MiB of HBM per device.

v0:
```python
import jax
import jax.numpy as jnp
from jax import lax
from jax.sharding import PartitionSpec as P


def shards(activations, kv_weight, pool_shrink, pool_expand, request_slot, slot_owner, slot_local):
    slot_count = slot_owner.shape[0]
    pool_count = pool_shrink.shape[0]
    rank_width = pool_shrink.shape[1]
    base_part = jnp.dot(activations, kv_weight, preferred_element_type=jnp.float32)
    owners = slot_owner[:, 0]
    local_rows = slot_local[:, 0]
    pool_row = owners * pool_count + local_rows
    pieces = (
        lax.all_gather(pool_shrink, "dp", axis=0, tiled=True),
        lax.all_gather(pool_expand, "dp", axis=0, tiled=True),
    )
    piece_rows = pieces[0].shape[0]
    chooser = (pool_row[:, None] == jnp.arange(piece_rows, dtype=jnp.int32)[None, :]).astype(
        jnp.bfloat16
    )
    slot_shrink = jnp.dot(
        chooser, pieces[0].reshape(piece_rows, -1), preferred_element_type=jnp.float32
    ).astype(jnp.bfloat16)
    slot_expand = jnp.dot(
        chooser, pieces[1].reshape(piece_rows, -1), preferred_element_type=jnp.float32
    ).astype(jnp.bfloat16)
    shrink_rows = slot_shrink.reshape(slot_count * rank_width, -1)
    expand_rows = slot_expand.reshape(slot_count * rank_width, -1)
    all_shrunk = lax.dot_general(
        activations, shrink_rows, (((1,), (1,)), ((), ())), preferred_element_type=jnp.float32
    )
    chosen = request_slot[:, None] == jnp.arange(slot_count, dtype=jnp.int32)[None, :]
    picked = jnp.where(
        chosen[:, :, None],
        all_shrunk.reshape(-1, slot_count, rank_width),
        jnp.zeros((), jnp.float32),
    )
    partial_shrunk = jnp.sum(picked, axis=1)
    shrunk = lax.psum(partial_shrunk, "tensor").astype(jnp.bfloat16)
    widened = jnp.where(
        chosen[:, :, None], shrunk[:, None, :], jnp.zeros((), jnp.bfloat16)
    ).reshape(-1, slot_count * rank_width)
    adapted = jnp.dot(widened, expand_rows, preferred_element_type=jnp.float32)
    base_total = lax.psum_scatter(base_part, "tensor", scatter_dimension=1, tiled=True)
    return (base_total + adapted).astype(jnp.bfloat16)


def solution(mesh):
    in_specs = (
        P("dp", "tensor"),
        P("tensor", None),
        P("dp", None, "tensor"),
        P("dp", None, "tensor"),
        P("dp"),
        P("dp", None),
        P("dp", None),
    )
    out_specs = P("dp", "tensor")
    return jax.shard_map(shards, mesh=mesh, in_specs=in_specs, out_specs=out_specs, check_vma=False)
```

profile of v0, /device:TPU:32, one launch (start us, length us, event | category | flops | bytes accessed | tf_op | source)
XLA Modules:
  0.0 278.7 jit_solution(7123384122963525590)
XLA Ops:
  7.4 0.0 copy-start
  7.4 0.0 all-gather.5.cloned.1.call-start
  7.4 0.7 all-gather.5.cloned.1.call-update
  8.1 0.0 all-gather.3.cloned.1.call-start
  8.1 0.7 all-gather.3.cloned.1.call-update
  8.8 0.0 reduce-scatter.2.cloned.1.call-start
  8.9 0.1 copy-done
  9.0 4.2 %fusion.5 = f32[512,2048]{1,0:T(8,128)} fusion(bf16[512,512]{1,0:T(8,128)(2,1)} %param.7, bf16[512,2048]{1,0:T(8,128)(2,1)S(1)} %copy-done), kind=kOutput, calls=%fused_computation.13 | convolution fusion | flops 1073741824 | bytes 6815744 | tf_op jit(solution)/shard_map/dot_general | solution.py:11
  13.2 0.0 reduce-scatter.2.cloned.1.call-update
  13.2 0.6 copy-done.3
  13.8 0.0 copy-done.4
  13.9 0.0 copy-done.2
  13.9 72.5 %all-gather.5.cloned.1.call-done = bf16[128,64,128]{2,1,0:T(8,128)(2,1)} async-done(((bf16[4,64,128]{2,1,0:T(8,128)(2,1)}), bf16[128,64,128]{2,1,0:T(8,128)(2,1)}) %all-gather.5.cloned.1.call-update) | async-done | bytes 2097168 | tf_op jit(solution)/shard_map/all_gather | solution.py:17
  86.4 2.9 %convolution_convert_fusion.1 = bf16[32,8192]{1,0:T(8,128)(2,1)S(1)} fusion(bf16[16,8,64,128]{3,2,1,0:T(8,128)(2,1)} %bitcast.23, s32[32]{0:T(128)S(1)} %add_bitcast_fusion), kind=kOutput, calls=%fused_computation.1 | convolution fusion | flops 67375104 | bytes 2621568 | tf_op jit(solution)/shard_map/dot_general | solution.py:26
  89.4 0.2 reshape.54
  89.6 75.6 %all-gather.3.cloned.1.call-done = bf16[128,64,512]{2,1,0:T(8,128)(2,1)} async-done(((bf16[4,64,512]{2,1,0:T(8,128)(2,1)}), bf16[128,64,512]{2,1,0:T(8,128)(2,1)}) %all-gather.3.cloned.1.call-update) | async-done | bytes 8388624 | tf_op jit(solution)/shard_map/all_gather | solution.py:16
  165.3 12.4 %copy.8 = bf16[16,8,64,512]{3,1,2,0:T(8,128)(2,1)} copy(bf16[16,8,64,512]{3,2,1,0:T(8,128)(2,1)} %bitcast.21) | data formatting | bytes 16777216
  177.7 6.0 %convolution_convert_fusion = bf16[32,32768]{1,0:T(8,128)(2,1)} fusion(bf16[128,32768]{1,0:T(8,128)(2,1)} %bitcast.19, s32[32]{0:T(128)S(1)} %add_bitcast_fusion), kind=kOutput, calls=%fused_computation | convolution fusion | flops 269488128 | bytes 10485888 | tf_op jit(solution)/shard_map/dot_general | solution.py:23
  183.7 4.2 %reshape.51 = bf16[2048,512]{1,0:T(8,128)(2,1)} reshape(bf16[32,32768]{1,0:T(8,128)(2,1)} %convolution_convert_fusion) | data formatting | bytes 4194304 | tf_op jit(solution)/shard_map/reshape | solution.py:29
  187.9 2.9 %fusion.6 = f32[2048,512]{1,0:T(8,128)S(1)} fusion(bf16[2048,512]{1,0:T(8,128)(2,1)} %reshape.51, bf16[512,512]{1,0:T(8,128)(2,1)S(1)} %copy-done.1), kind=kOutput, calls=%fused_computation.14 | convolution fusion | flops 1073741824 | bytes 6815744 | tf_op jit(solution)/shard_map/dot_general | solution.py:31
  190.9 0.6 select_reduce_fusion
  191.5 75.3 %all-reduce.1 = bf16[512,64]{0,1:T(8,128)(2,1)S(1)} all-reduce(f32[512,64]{0,1:T(8,128)S(1)} %select_reduce_fusion), channel_id=1, replica_groups=mesh['dp'=32,'tensor'=16] {'tensor'}, use_global_device_ids=true, to_apply=%region_2.3 | all-reduce | flops 32768 | bytes 196608 | tf_op jit(solution)/shard_map/psum | solution.py:41
  266.8 1.5 broadcast_select_fusion
  268.2 3.0 %fusion.2 = bf16[512,128]{1,0:T(8,128)(2,1)} fusion(f32[512,128]{1,0:T(8,128)} %reduce-scatter.2.cloned.1.call-done, bf16[512,2048]{0,1:T(8,128)(2,1)} %bitcast.22, bf16[2048,128]{1,0:T(8,128)(2,1)S(1)} %reshape.54), kind=kOutput, calls=%fused_computation.7 | convolution fusion | flops 268566528 | bytes 3014656 | tf_op jit(solution)/shard_map/dot_general | solution.py:45
  (8 shorter events, 0.0 us)
Async XLA Ops:
  7.4 1.6 copy-start
  7.4 79.1 %all-gather.5.cloned.1.call-start = ((), (), s32[]{:S(2)}) async-start(), calls=%async_computation.3 | async-start | bytes 2162688 | tf_op jit(solution)/shard_map/all_gather | solution.py:17
  8.1 157.2 %all-gather.3.cloned.1.call-start = ((), (), s32[]{:S(2)}) async-start(), calls=%async_computation.2 | async-start | bytes 8650752 | tf_op jit(solution)/shard_map/all_gather | solution.py:16
  8.8 259.4 %reduce-scatter.2.cloned.1.call-start = ((), (), s32[]{:S(2)}) async-start(), calls=%async_computation.1 | async-start | bytes 4456448 | tf_op jit(solution)/shard_map/reduce_scatter | solution.py:46
  13.2 0.7 copy-start.3
  13.2 0.7 copy-start.4
  13.2 0.7 copy-start.2
  183.7 4.3 %copy-start.1 = (bf16[512,512]{1,0:T(8,128)(2,1)S(1)}, bf16[512,512]{1,0:T(8,128)(2,1)}, u32[]{:S(2)}) copy-start(bf16[512,512]{1,0:T(8,128)(2,1)} %param.7) | copy-start | bytes 1572868
Sparse Core Ops, SparseCore 0:
  10.5 75.8 all-gather.4
  88.8 76.4 all-gather.2
Sparse Core Ops, SparseCore 1:
  13.5 97.1 reduce-scatter.1
where the time goes:
time: 279 us
  waiting for transfers between devices  150 us (54%)
  blocking collectives  75.3 us (27%)
  matrix products  19.1 us (7%)
  local copies, waits for them, and re-layouts  17.7 us (6%)
  between operations  14.9 us (5%)
    all_gather x1, waiting for transfers between devices, shards(): lax.all_gather(pool_shrink, 'dp', axis=0, tiled=True)  75.6 us
    psum x1, blocking collectives, shards(): shrunk = lax.psum(partial_shrunk, 'tensor').astype(jnp.bfloat16)  75.3 us
    all_gather x1, waiting for transfers between devices, shards(): lax.all_gather(pool_expand, 'dp', axis=0, tiled=True)  72.5 us
    unnamed x11, local copies, waits for them, and re-layouts  13.2 us
    dot_general x1, matrix products, shards(): jnp.dot(chooser, pieces[0].reshape(piece_rows, -1), preferred_element_typ...  5.99 us
  transfers between devices with their start and end apart: 3, of which 2 were waited for; matrix products, arithmetic and copies ran while one was open for 13% of the time, Pallas kernels for 0%

commit v1 on v0

v1 whole, which is shorter than its diff:
```python
import functools

import jax
import jax.numpy as jnp
from jax import lax
from jax.experimental import pallas as pl
from jax.experimental.pallas import tpu as pltpu
from jax.sharding import PartitionSpec as P

MESH = pl.DeviceIdType.MESH
BF16, F32 = jnp.bfloat16, jnp.float32
PLANES, CORES, XS, YS = 16, 2, 4, 4
OWNERS, PEERS = PLANES * CORES, XS * YS
HELD, RANK, SLOTS = 4, 64, 32
REQ, WIDTH, FEAT = 512, 512, 128
HALF = PLANES // 2
ORDERS = ((0, 1, 2, 3), (2, 3, 0, 1))
KEPT = ((0, 1), (2, 3))
EXPAND_LATE = 5


def away(offset):
    return sum(min(step, 4 - step) for step in offset)


OFFSETS = sorted(((i, j) for i in range(XS) for j in range(YS) if i or j), key=lambda offset: -away(offset))


def remote(src, dst, send, recv, device):
    return pltpu.make_async_remote_copy(
        src_ref=src, dst_ref=dst, send_sem=send, recv_sem=recv, device_id=device, device_id_type=MESH
    )


def kernel(
    owners, locals_, slots, act_hbm, kv_hbm, shrink_hbm, expand_hbm, out,
    act, act_t, kv, shrinks, expands, part_out, part_in, base, adapter, picked, sum_in, sum_own, shrunk_t, hot, rows,
    load, ring_send, ring_recv, sib_send, sib_recv, up_send, up_recv, upsib_send, upsib_recv,
    base_send, base_recv, sum_send, sum_recv, all_send, all_recv,
):
    dp, tensor = lax.axis_index("dp"), lax.axis_index("tensor")
    z, core = dp // CORES, dp % CORES
    x, y = tensor // YS, tensor % YS

    def owner_at(way, hop, which=core):
        plane = (z - hop + PLANES) % PLANES if way == 0 else (z + hop) % PLANES
        return plane * CORES + which

    next_of = ({"dp": owner_at(1, 1)}, {"dp": owner_at(0, 1)})
    sibling = {"dp": z * CORES + 1 - core}

    def peer(offset, sign=1):
        other_x = (x + sign * offset[0] + XS) % XS
        other_y = (y + sign * offset[1] + YS) % YS
        return other_x, other_y

    def peer_id(offset, sign=1):
        other_x, other_y = peer(offset, sign)
        return {"tensor": other_x * YS + other_y}

    loads = [
        pltpu.make_async_copy(act_hbm, act, load.at[0]),
        pltpu.make_async_copy(kv_hbm, kv, load.at[1]),
        pltpu.make_async_copy(shrink_hbm, shrinks.at[dp], load.at[2]),
        pltpu.make_async_copy(expand_hbm, expands.at[dp], load.at[3]),
    ]
    for copy in loads:
        copy.start()

    barrier = pltpu.get_barrier_semaphore()
    for device in (next_of[0], next_of[1], sibling):
        pl.semaphore_signal(barrier, inc=1, device_id=device, device_id_type=MESH)
    for offset in OFFSETS:
        pl.semaphore_signal(barrier, inc=1, device_id=peer_id(offset), device_id_type=MESH)
    pl.semaphore_wait(barrier, 3 + len(OFFSETS))

    def ring_copy(way, hop, chunk, src):
        return remote(
            src, shrinks.at[owner_at(way, hop), chunk], ring_send.at[way, hop, chunk],
            ring_recv.at[way, hop, chunk], next_of[way],
        )

    def ring_forward(way, hop, chunk):
        ring_copy(way, hop, chunk, shrinks.at[owner_at(way, hop), chunk]).start()

    def ring_arrived(way, hop, chunk):
        owner = owner_at(way, hop)
        remote(
            shrinks.at[owner, chunk], shrinks.at[owner, chunk], ring_send.at[way, hop, chunk],
            ring_recv.at[way, hop - 1, chunk], next_of[way],
        ).wait_recv()

    def sib_copy(way, hop, which):
        shard = shrinks.at[owner_at(way, hop, which)]
        return remote(shard, shard, sib_send.at[way, hop], sib_recv.at[way, hop], sibling)

    def sib_half(way, which):
        shard = shrinks.at[owner_at(way, HALF, which), pl.ds(2 * way, 2)]
        return remote(shard, shard, sib_send.at[way, HALF], sib_recv.at[way, HALF], sibling)

    def up_part(way, hop):
        return pl.ds(2 * way, 2) if hop == HALF else pl.ds(0, HELD)

    def up_copy(way, hop, owner, piece):
        part = expands.at[owner, pl.ds(2 * piece, 2)]
        return remote(part, part, up_send.at[way, hop, piece], up_recv.at[way, hop, piece], next_of[way])

    def up_forward(way, hop):
        for piece in (way, 1 - way):
            if hop < HALF - 1 or piece == way:
                up_copy(way, hop, owner_at(way, hop), piece).start()

    def upsib_copy(way, hop, which):
        shard = expands.at[owner_at(way, hop, which), up_part(way, hop)]
        return remote(shard, shard, upsib_send.at[way, hop], upsib_recv.at[way, hop], sibling)

    def up_hop(hop):
        for way in (0, 1):
            for piece in (way, 1 - way):
                if hop < HALF or piece == way:
                    up_copy(way, hop - 1, owner_at(way, hop), piece).wait_recv()
                    if hop < HALF - 1 or (hop == HALF - 1 and piece == way):
                        up_copy(way, hop, owner_at(way, hop), piece).start()
            upsib_copy(way, hop, core).start()

    for place in range(HELD):
        for way in (0, 1):
            chunk = ORDERS[way][place]
            ring_copy(way, 0, chunk, shrink_hbm.at[chunk]).start()

    loads[0].wait()
    loads[1].wait()

    def base_block(pair, carry):
        both = jnp.dot(act[...], kv[:, pl.ds(pl.multiple_of(pair * 2 * FEAT, 2 * FEAT), 2 * FEAT)], preferred_element_type=F32)
        part_out[2 * pair] = both[:, :FEAT].astype(BF16)
        part_out[2 * pair + 1] = both[:, FEAT:].astype(BF16)
        return carry

    lax.fori_loop(0, PEERS // 2, base_block, 0)

    def base_copy(index):
        offset = OFFSETS[index]
        other_x, other_y = peer(offset)
        return remote(
            part_out.at[other_x * YS + other_y], part_in.at[index], base_send.at[index], base_recv.at[index], peer_id(offset)
        )

    for index in range(len(OFFSETS)):
        base_copy(index).start()
    base[...] = jnp.dot(
        act[...], kv[:, pl.ds(pl.multiple_of(tensor * FEAT, FEAT), FEAT)], preferred_element_type=F32
    )

    loads[2].wait()
    loads[3].wait()
    sib_copy(0, 0, core).start()
    slot_row = slots[...]
    named = jnp.zeros((1, REQ), jnp.int32)
    for slot in range(SLOTS):
        named = jnp.where(slot_row == slot, owners[slot] * HELD + locals_[slot], named)
    adapter[...] = jnp.broadcast_to(named, adapter.shape)
    act_t[...] = act[...].T
    slot_column = jnp.broadcast_to(slot_row, (FEAT, REQ)).T
    lane_slot = lax.broadcasted_iota(jnp.int32, (REQ, FEAT), 1) // RANK
    for pair in range(SLOTS // 2):
        hot[:, pair * FEAT : (pair + 1) * FEAT] = jnp.where(slot_column == lane_slot + 2 * pair, 1.0, 0.0).astype(BF16)
    picked[...] = jnp.zeros_like(picked)

    def shrink_with(owner, first=0, count=HELD):
        weights = shrinks[owner, pl.ds(first, count)].reshape(count * RANK, WIDTH)
        block = jnp.dot(weights, act_t[...], preferred_element_type=F32)
        total = picked[...]
        for local in range(count):
            hit = adapter[0:1, :] == owner * HELD + first + local
            total = jnp.where(hit, block[local * RANK : (local + 1) * RANK], total)
        picked[...] = total

    def add_base(index):
        base_copy(index).wait_recv()
        base[...] += part_in[index].astype(F32)

    def work(place, hop):
        way = place % 2
        if place < 2:
            shrink_with(owner_at(way, hop))
        elif way == 0:
            sib_copy(0, hop, 1 - core).wait_recv()
            shrink_with(owner_at(0, hop, 1 - core))
        else:
            @pl.when(hop > 0)
            def _():
                sib_copy(1, hop, 1 - core).wait_recv()

            shrink_with(owner_at(1, hop, 1 - core))

    def shrink_hop(hop, carry):
        for place in range(HELD):
            for way in (0, 1):
                chunk = ORDERS[way][place]
                ring_arrived(way, hop, chunk)
                if chunk in KEPT[way]:
                    ring_forward(way, hop, chunk)
                else:
                    pl.when(hop < HALF - 1)(functools.partial(ring_forward, way, hop, chunk))
            work(place, hop - 1)
        for way in (0, 1):
            sib_copy(way, hop, core).start()
        return carry

    lax.fori_loop(1, 4, shrink_hop, 0)
    up_forward(0, 0)
    up_forward(1, 0)
    upsib_copy(0, 0, core).start()
    for hop in range(4, HALF):
        shrink_hop(hop, 0)
        up_hop(hop - 3)
        if hop >= 5:
            for index in range(5 * (hop - 5), 5 * (hop - 4)):
                add_base(index)
    for place in (0, 1):
        for way in (0, 1):
            ring_arrived(way, HALF, ORDERS[way][place])
    for way in (0, 1):
        sib_half(way, core).start()
    up_hop(EXPAND_LATE)
    for place in range(HELD):
        work(place, HALF - 1)
    for way in (0, 1):
        shrink_with(owner_at(way, HALF), 2 * way, 2)
    for way in (0, 1):
        sib_half(way, 1 - core).wait_recv()
        shrink_with(owner_at(way, HALF, 1 - core), 2 * way, 2)

    def piece_of(ref, at_x, at_y):
        return ref.at[pl.ds(pl.multiple_of(at_x * 16, 16), 16), pl.ds(pl.multiple_of(at_y * 128, 128), 128)]

    def sum_copy(index):
        other_x, other_y = peer(OFFSETS[index])
        return remote(
            piece_of(picked, other_x, other_y), sum_in.at[index], sum_send.at[index], sum_recv.at[index], peer_id(OFFSETS[index])
        )

    def all_copy(index, sign=1):
        at_x, at_y = (x, y) if sign == 1 else peer(OFFSETS[index], -1)
        return remote(
            piece_of(shrunk_t, at_x, at_y), piece_of(shrunk_t, at_x, at_y), all_send.at[index], all_recv.at[index],
            peer_id(OFFSETS[index]),
        )

    for index in range(len(OFFSETS)):
        sum_copy(index).start()
    up_hop(6)
    total = piece_of(picked, x, y)[...]
    for index in reversed(range(len(OFFSETS))):
        sum_copy(index).wait_recv()
        total += sum_in[index]
    piece_of(shrunk_t, x, y)[...] = total.astype(BF16)
    for index in range(len(OFFSETS)):
        all_copy(index).start()
    up_hop(7)
    for index in reversed(range(len(OFFSETS))):
        all_copy(index, -1).wait_recv()
    twice = jnp.concatenate([shrunk_t[...], shrunk_t[...]], axis=0).T
    for pair in range(SLOTS // 2):
        hot[:, pair * FEAT : (pair + 1) * FEAT] *= twice
    up_hop(HALF)
    upsib_copy(0, 0, 1 - core).wait_recv()
    for hop in range(1, HALF + 1):
        for way in (0, 1):
            upsib_copy(way, hop, 1 - core).wait_recv()
    for slot in range(SLOTS):
        rows[slot * RANK : (slot + 1) * RANK, :] = expands[owners[slot], locals_[slot]]
    out[...] = (base[...] + jnp.dot(hot[...], rows[...], preferred_element_type=F32)).astype(BF16)

    for way in (0, 1):
        for hop in range(HALF):
            for chunk in range(HELD):
                if hop < HALF - 1 or chunk in KEPT[way]:
                    ring_copy(way, hop, chunk, shrinks.at[owner_at(way, hop), chunk]).wait_send()
            for piece in (0, 1):
                if hop < HALF - 1 or piece == way:
                    up_copy(way, hop, owner_at(way, hop), piece).wait_send()
        for hop in range(HALF + 1):
            if hop or way == 0:
                (sib_half(way, core) if hop == HALF else sib_copy(way, hop, core)).wait_send()
                upsib_copy(way, hop, core).wait_send()
    for index in range(len(OFFSETS)):
        base_copy(index).wait_send()
        sum_copy(index).wait_send()
        all_copy(index).wait_send()


def shards(activations, kv_weight, pool_shrink, pool_expand, request_slot, slot_owner, slot_local):
    peers = len(OFFSETS)
    dma = pltpu.SemaphoreType.DMA
    hbm = pl.BlockSpec(memory_space=pl.ANY)
    smem = pl.BlockSpec(memory_space=pltpu.SMEM)
    vmem = pl.BlockSpec(memory_space=pltpu.VMEM)
    return pl.pallas_call(
        kernel,
        out_shape=jax.ShapeDtypeStruct((REQ, FEAT), BF16),
        in_specs=[smem, smem, vmem, hbm, hbm, hbm, hbm],
        out_specs=vmem,
        scratch_shapes=[
            pltpu.VMEM((REQ, WIDTH), BF16),
            pltpu.VMEM((WIDTH, REQ), BF16),
            pltpu.VMEM((WIDTH, PEERS * FEAT), BF16),
            pltpu.VMEM((OWNERS, HELD, RANK, WIDTH), BF16),
            pltpu.VMEM((OWNERS, HELD, RANK, FEAT), BF16),
            pltpu.VMEM((PEERS, REQ, FEAT), BF16),
            pltpu.VMEM((peers, REQ, FEAT), BF16),
            pltpu.VMEM((REQ, FEAT), F32),
            pltpu.VMEM((8, REQ), jnp.int32),
            pltpu.VMEM((RANK, REQ), F32),
            pltpu.VMEM((peers, 16, 128), F32),
            pltpu.VMEM((16, 128), F32),
            pltpu.VMEM((RANK, REQ), BF16),
            pltpu.VMEM((REQ, SLOTS * RANK), BF16),
            pltpu.VMEM((SLOTS * RANK, FEAT), BF16),
            dma((4,)),
            dma((2, HALF, HELD)),
            dma((2, HALF, HELD)),
            dma((2, HALF + 1)),
            dma((2, HALF + 1)),
            dma((2, HALF, 2)),
            dma((2, HALF, 2)),
            dma((2, HALF + 1)),
            dma((2, HALF + 1)),
            dma((peers,)),
            dma((peers,)),
            dma((peers,)),
            dma((peers,)),
            dma((peers,)),
            dma((peers,)),
        ],
        compiler_params=pltpu.CompilerParams(
            collective_id=0, has_side_effects=True, vmem_limit_bytes=40 * 2**20
        ),
    )(
        slot_owner.reshape(-1), slot_local.reshape(-1), request_slot.reshape(1, -1),
        activations, kv_weight, pool_shrink, pool_expand,
    )


def solution(mesh):
    in_specs = (
        P("dp", "tensor"),
        P("tensor", None),
        P("dp", None, "tensor"),
        P("dp", None, "tensor"),
        P("dp"),
        P("dp", None),
        P("dp", None),
    )
    out_specs = P("dp", "tensor")
    return jax.shard_map(shards, mesh=mesh, in_specs=in_specs, out_specs=out_specs, check_vma=False)
```

time: 279 us -> 91.5 us (0.33)
  the two profiles are of different devices: /device:TPU:32 before, /device:TPU:1 now
where the time goes in v1:
time: 91.5 us; the launch traced here: 91.2 us
  Pallas kernels  84.1 us (92%)
  local copies, waits for them, and re-layouts  7.07 us (8%)
    pallas_call x1, Pallas kernels, shards(): pl.pallas_call(kernel, out_shape=jax.ShapeDtypeStruct((REQ, FEAT), BF16),...  84.1 us
    unnamed x15, local copies, waits for them, and re-layouts  7.07 us

profile of v1, /device:TPU:1, one launch (start us, length us, event | category | flops | bytes accessed | tf_op | source)
XLA Modules:
  0.0 91.2 jit_solution(7559909405345420599)
XLA Ops:
  0.0 0.0 copy-start
  0.0 1.6 %copy-done = bf16[512,2048]{1,0:T(8,128)(2,1)S(1)} copy-done((bf16[512,2048]{1,0:T(8,128)(2,1)S(1)}, bf16[512,2048]{1,0:T(8,128)(2,1)}, u32[]{:S(2)}) %copy-start) | copy-done | bytes 2097176
  1.6 0.0 copy-start.1
  1.6 1.0 %copy-done.1 = bf16[512,512]{1,0:T(8,128)(2,1)S(1)} copy-done((bf16[512,512]{1,0:T(8,128)(2,1)S(1)}, bf16[512,512]{1,0:T(8,128)(2,1)}, u32[]{:S(2)}) %copy-start.1) | copy-done | bytes 524312
  2.6 0.0 copy-start.2
  2.6 0.9 %copy-done.2 = bf16[4,64,512]{2,1,0:T(8,128)(2,1)S(1)} copy-done((bf16[4,64,512]{2,1,0:T(8,128)(2,1)S(1)}, bf16[4,64,512]{2,1,0:T(8,128)(2,1)}, u32[]{:S(2)}) %copy-start.2) | copy-done | bytes 262168
  3.6 0.0 copy-start.3
  3.6 0.8 copy-done.3
  4.4 0.0 copy-start.4
  4.4 0.7 copy-done.4
  5.1 0.0 copy-start.5
  5.1 0.7 copy-done.5
  5.8 0.0 copy-start.6
  5.8 0.7 copy-done.6
  6.4 84.1 %shard_map.73 = bf16[512,128]{1,0:T(8,128)(2,1)S(1)} custom-call(s32[32]{0:T(128)S(1)} %bitcast.4, s32[32]{0:T(128)S(1)} %bitcast.5, s32[1,512]{1,0:T(1,128)S(1)} %bitcast.3, bf16[512,512]{1,0:T(8,128)(2,1)S(1)} %copy-done.1, bf16[512,2048]{1,0:T(8,128)(2,1)S(1)} %copy-done, bf16[4,64,512]{2,1,0:T(8,128)(2,1)S(1)} %copy-done.2, bf16[4,64,128]{2,1,0:T(8,128)(2,1)S(1)} %copy-done.3), custom_call_target="tpu_custom_call" | custom-call | tf_op jit(solution)/shard_map/pallas_call | solution.py:300
  90.5 0.7 copy.9
Async XLA Ops:
  0.0 1.6 %copy-start = (bf16[512,2048]{1,0:T(8,128)(2,1)S(1)}, bf16[512,2048]{1,0:T(8,128)(2,1)}, u32[]{:S(2)}) copy-start(bf16[512,2048]{1,0:T(8,128)(2,1)} %kv_hbm.1) | copy-start | bytes 6291460
  1.6 1.0 %copy-start.1 = (bf16[512,512]{1,0:T(8,128)(2,1)S(1)}, bf16[512,512]{1,0:T(8,128)(2,1)}, u32[]{:S(2)}) copy-start(bf16[512,512]{1,0:T(8,128)(2,1)} %act_hbm.1) | copy-start | bytes 1572868
  2.6 0.9 %copy-start.2 = (bf16[4,64,512]{2,1,0:T(8,128)(2,1)S(1)}, bf16[4,64,512]{2,1,0:T(8,128)(2,1)}, u32[]{:S(2)}) copy-start(bf16[4,64,512]{2,1,0:T(8,128)(2,1)} %shrink_hbm.1) | copy-start | bytes 786436
  3.6 0.8 copy-start.3
  4.4 0.7 copy-start.4
  5.1 0.7 copy-start.5
  5.8 0.7 copy-start.6

commit v2 on v1

--- a/solution.py
+++ b/solution.py
@@ -16,7 +16,7 @@
 HALF = PLANES // 2
 ORDERS = ((0, 1, 2, 3), (2, 3, 0, 1))
 KEPT = ((0, 1), (2, 3))
-EXPAND_LATE = 5
+EXPAND_LATE = 4
 
 
 def away(offset):
@@ -33,8 +33,8 @@
 
 
 def kernel(
-    owners, locals_, slots, act_hbm, kv_hbm, shrink_hbm, expand_hbm, out,
-    act, act_t, kv, shrinks, expands, part_out, part_in, base, adapter, picked, sum_in, sum_own, shrunk_t, hot, rows,
+    owners_hbm, locals_hbm, slots_hbm, act_hbm, kv_hbm, shrink_hbm, expand_hbm, out,
+    owners, locals_, slots, act, act_t, kv, shrinks, expands, part_out, part_in, base, adapter, picked, sum_in, shrunk_t, hot, rows,
     load, ring_send, ring_recv, sib_send, sib_recv, up_send, up_recv, upsib_send, upsib_recv,
     base_send, base_recv, sum_send, sum_recv, all_send, all_recv,
 ):
@@ -47,6 +47,7 @@
         return plane * CORES + which
 
     next_of = ({"dp": owner_at(1, 1)}, {"dp": owner_at(0, 1)})
+    after_next = ({"dp": owner_at(1, 2)}, {"dp": owner_at(0, 2)})
     sibling = {"dp": z * CORES + 1 - core}
 
     def peer(offset, sign=1):
@@ -63,16 +64,18 @@
         pltpu.make_async_copy(kv_hbm, kv, load.at[1]),
         pltpu.make_async_copy(shrink_hbm, shrinks.at[dp], load.at[2]),
         pltpu.make_async_copy(expand_hbm, expands.at[dp], load.at[3]),
+        pltpu.make_async_copy(owners_hbm, owners, load.at[4]),
+        pltpu.make_async_copy(locals_hbm, locals_, load.at[5]),
+        pltpu.make_async_copy(slots_hbm, slots, load.at[6]),
     ]
-    for copy in loads:
-        copy.start()
-
     barrier = pltpu.get_barrier_semaphore()
-    for device in (next_of[0], next_of[1], sibling):
+    for device in (*next_of, *after_next, sibling):
         pl.semaphore_signal(barrier, inc=1, device_id=device, device_id_type=MESH)
     for offset in OFFSETS:
         pl.semaphore_signal(barrier, inc=1, device_id=peer_id(offset), device_id_type=MESH)
-    pl.semaphore_wait(barrier, 3 + len(OFFSETS))
+    for copy in loads:
+        copy.start()
+    pl.semaphore_wait(barrier, 5 + len(OFFSETS))
 
     def ring_copy(way, hop, chunk, src):
         return remote(
@@ -101,14 +104,26 @@
     def up_part(way, hop):
         return pl.ds(2 * way, 2) if hop == HALF else pl.ds(0, HELD)
 
-    def up_copy(way, hop, owner, piece):
+    def up_copy(way, hop, owner, piece, step=1):
         part = expands.at[owner, pl.ds(2 * piece, 2)]
-        return remote(part, part, up_send.at[way, hop, piece], up_recv.at[way, hop, piece], next_of[way])
+        device = next_of[way] if step == 1 else after_next[way]
+        return remote(part, part, up_send.at[way, hop, piece, step - 1], up_recv.at[way, hop + step - 1, piece], device)
+
+    def up_sends(way, hop, piece):
+        if hop < EXPAND_LATE:
+            steps = (1,)
+        elif (hop - EXPAND_LATE) % 2 == 0:
+            steps = (2, 1)
+        else:
+            steps = ()
+        for step in steps:
+            if hop + step < HALF or (hop + step == HALF and piece == way):
+                yield up_copy(way, hop, owner_at(way, hop), piece, step)
 
     def up_forward(way, hop):
         for piece in (way, 1 - way):
-            if hop < HALF - 1 or piece == way:
-                up_copy(way, hop, owner_at(way, hop), piece).start()
+            for copy in up_sends(way, hop, piece):
+                copy.start()
 
     def upsib_copy(way, hop, which):
         shard = expands.at[owner_at(way, hop, which), up_part(way, hop)]
@@ -119,8 +134,8 @@
             for piece in (way, 1 - way):
                 if hop < HALF or piece == way:
                     up_copy(way, hop - 1, owner_at(way, hop), piece).wait_recv()
-                    if hop < HALF - 1 or (hop == HALF - 1 and piece == way):
-                        up_copy(way, hop, owner_at(way, hop), piece).start()
+                    for copy in up_sends(way, hop, piece):
+                        copy.start()
             upsib_copy(way, hop, core).start()
 
     for place in range(HELD):
@@ -152,8 +167,8 @@
         act[...], kv[:, pl.ds(pl.multiple_of(tensor * FEAT, FEAT), FEAT)], preferred_element_type=F32
     )
 
-    loads[2].wait()
-    loads[3].wait()
+    for copy in loads[2:]:
+        copy.wait()
     sib_copy(0, 0, core).start()
     slot_row = slots[...]
     named = jnp.zeros((1, REQ), jnp.int32)
@@ -208,24 +223,22 @@
             sib_copy(way, hop, core).start()
         return carry
 
-    lax.fori_loop(1, 4, shrink_hop, 0)
+    lax.fori_loop(1, 5, shrink_hop, 0)
     up_forward(0, 0)
     up_forward(1, 0)
     upsib_copy(0, 0, core).start()
-    for hop in range(4, HALF):
+    for hop in range(5, HALF):
         shrink_hop(hop, 0)
-        up_hop(hop - 3)
-        if hop >= 5:
-            for index in range(5 * (hop - 5), 5 * (hop - 4)):
-                add_base(index)
-    for place in (0, 1):
-        for way in (0, 1):
+        up_hop(hop - 4)
+        for index in range(5 * (hop - 5), 5 * (hop - 4)):
+            add_base(index)
+    for place in range(HELD):
+        work(place, HALF - 1)
+    for way in (0, 1):
+        for place in (0, 1):
             ring_arrived(way, HALF, ORDERS[way][place])
-    for way in (0, 1):
         sib_half(way, core).start()
     up_hop(EXPAND_LATE)
-    for place in range(HELD):
-        work(place, HALF - 1)
     for way in (0, 1):
         shrink_with(owner_at(way, HALF), 2 * way, 2)
     for way in (0, 1):
@@ -251,6 +264,7 @@
     for index in range(len(OFFSETS)):
         sum_copy(index).start()
     up_hop(6)
+    up_hop(5)
     total = piece_of(picked, x, y)[...]
     for index in reversed(range(len(OFFSETS))):
         sum_copy(index).wait_recv()
@@ -258,12 +272,12 @@
     piece_of(shrunk_t, x, y)[...] = total.astype(BF16)
     for index in range(len(OFFSETS)):
         all_copy(index).start()
-    up_hop(7)
     for index in reversed(range(len(OFFSETS))):
         all_copy(index, -1).wait_recv()
     twice = jnp.concatenate([shrunk_t[...], shrunk_t[...]], axis=0).T
     for pair in range(SLOTS // 2):
         hot[:, pair * FEAT : (pair + 1) * FEAT] *= twice
+    up_hop(7)
     up_hop(HALF)
     upsib_copy(0, 0, 1 - core).wait_recv()
     for hop in range(1, HALF + 1):
@@ -279,8 +293,8 @@
                 if hop < HALF - 1 or chunk in KEPT[way]:
                     ring_copy(way, hop, chunk, shrinks.at[owner_at(way, hop), chunk]).wait_send()
             for piece in (0, 1):
-                if hop < HALF - 1 or piece == way:
-                    up_copy(way, hop, owner_at(way, hop), piece).wait_send()
+                for copy in up_sends(way, hop, piece):
+                    copy.wait_send()
         for hop in range(HALF + 1):
             if hop or way == 0:
                 (sib_half(way, core) if hop == HALF else sib_copy(way, hop, core)).wait_send()
@@ -294,15 +308,17 @@
 def shards(activations, kv_weight, pool_shrink, pool_expand, request_slot, slot_owner, slot_local):
     peers = len(OFFSETS)
     dma = pltpu.SemaphoreType.DMA
-    hbm = pl.BlockSpec(memory_space=pl.ANY)
-    smem = pl.BlockSpec(memory_space=pltpu.SMEM)
+    hbm = pl.BlockSpec(memory_space=pltpu.HBM)
     vmem = pl.BlockSpec(memory_space=pltpu.VMEM)
     return pl.pallas_call(
         kernel,
         out_shape=jax.ShapeDtypeStruct((REQ, FEAT), BF16),
-        in_specs=[smem, smem, vmem, hbm, hbm, hbm, hbm],
+        in_specs=[hbm] * 7,
         out_specs=vmem,
         scratch_shapes=[
+            pltpu.SMEM((SLOTS,), jnp.int32),
+            pltpu.SMEM((SLOTS,), jnp.int32),
+            pltpu.VMEM((1, REQ), jnp.int32),
             pltpu.VMEM((REQ, WIDTH), BF16),
             pltpu.VMEM((WIDTH, REQ), BF16),
             pltpu.VMEM((WIDTH, PEERS * FEAT), BF16),
@@ -314,16 +330,15 @@
             pltpu.VMEM((8, REQ), jnp.int32),
             pltpu.VMEM((RANK, REQ), F32),
             pltpu.VMEM((peers, 16, 128), F32),
-            pltpu.VMEM((16, 128), F32),
             pltpu.VMEM((RANK, REQ), BF16),
             pltpu.VMEM((REQ, SLOTS * RANK), BF16),
             pltpu.VMEM((SLOTS * RANK, FEAT), BF16),
-            dma((4,)),
+            dma((7,)),
             dma((2, HALF, HELD)),
             dma((2, HALF, HELD)),
             dma((2, HALF + 1)),
             dma((2, HALF + 1)),
-            dma((2, HALF, 2)),
+            dma((2, HALF, 2, 2)),
             dma((2, HALF, 2)),
             dma((2, HALF + 1)),
             dma((2, HALF + 1)),
@@ -335,7 +350,7 @@
             dma((peers,)),
         ],
         compiler_params=pltpu.CompilerParams(
-            collective_id=0, has_side_effects=True, vmem_limit_bytes=40 * 2**20
+            collective_id=0, has_side_effects=True, vmem_limit_bytes=60 * 2**20
         ),
     )(
         slot_owner.reshape(-1), slot_local.reshape(-1), request_slot.reshape(1, -1),

time: 91.5 us -> 84.4 us (0.922)
  local copies, waits for them, and re-layouts: 7.07 us -> 1.57 us
  Pallas kernels: 84.1 us -> 82.7 us
    unnamed x15 -> x1, local copies, waits for them, and re-layouts: 7.07 us -> 1.57 us
    pallas_call x1, Pallas kernels: 84.1 us -> 82.7 us  [shards(): pl.pallas_call(kernel, out_shape=jax.ShapeDtypeStruct((REQ, FEAT), BF16),...]
where the time goes in v2:
time: 84.4 us; the launch traced here: 84.3 us
  Pallas kernels  82.7 us (98%)
  local copies, waits for them, and re-layouts  1.57 us (2%)
    pallas_call x1, Pallas kernels, shards(): pl.pallas_call(kernel, out_shape=jax.ShapeDtypeStruct((REQ, FEAT), BF16),...  82.7 us

profile of v2, /device:TPU:1, one launch (start us, length us, event | category | flops | bytes accessed | tf_op | source)
XLA Modules:
  0.0 84.3 jit_solution(8638895665490685281)
XLA Ops:
  0.0 82.7 %shard_map.73 = bf16[512,128]{1,0:T(8,128)(2,1)} custom-call(s32[32]{0:T(128)} %bitcast.4, s32[32]{0:T(128)} %bitcast.5, s32[1,512]{1,0:T(1,128)} %bitcast.3, bf16[512,512]{1,0:T(8,128)(2,1)} %act_hbm.1, bf16[512,2048]{1,0:T(8,128)(2,1)} %kv_hbm.1, bf16[4,64,512]{2,1,0:T(8,128)(2,1)} %shrink_hbm.1, bf16[4,64,128]{2,1,0:T(8,128)(2,1)} %expand_hbm.1), custom_call_target="tpu_custom_call" | custom-call | tf_op jit(solution)/shard_map/pallas_call | solution.py:313
  82.7 1.6 %copy.9 = bf16[512,128]{1,0:T(8,128)(2,1)} copy(bf16[512,128]{1,0:T(8,128)(2,1)} %shard_map.73) | data formatting | bytes 262144

commit v3 on v2

--- a/solution.py
+++ b/solution.py
@@ -129,30 +129,39 @@
         shard = expands.at[owner_at(way, hop, which), up_part(way, hop)]
         return remote(shard, shard, upsib_send.at[way, hop], upsib_recv.at[way, hop], sibling)
 
+    def up_arrived(hop, turn):
+        for way in (0, 1):
+            piece = way if turn == 0 else 1 - way
+            if hop < HALF or turn == 0:
+                up_copy(way, hop - 1, owner_at(way, hop), piece).wait_recv()
+                for copy in up_sends(way, hop, piece):
+                    copy.start()
+
+    def up_shared(hop):
+        for way in (0, 1):
+            upsib_copy(way, hop, core).start()
+
     def up_hop(hop):
-        for way in (0, 1):
-            for piece in (way, 1 - way):
-                if hop < HALF or piece == way:
-                    up_copy(way, hop - 1, owner_at(way, hop), piece).wait_recv()
-                    for copy in up_sends(way, hop, piece):
-                        copy.start()
-            upsib_copy(way, hop, core).start()
+        for turn in (0, 1):
+            up_arrived(hop, turn)
+        up_shared(hop)
 
     for place in range(HELD):
         for way in (0, 1):
             chunk = ORDERS[way][place]
             ring_copy(way, 0, chunk, shrink_hbm.at[chunk]).start()
 
-    loads[0].wait()
-    loads[1].wait()
-
-    def base_block(pair, carry):
+    def base_block(pair):
         both = jnp.dot(act[...], kv[:, pl.ds(pl.multiple_of(pair * 2 * FEAT, 2 * FEAT), 2 * FEAT)], preferred_element_type=F32)
         part_out[2 * pair] = both[:, :FEAT].astype(BF16)
         part_out[2 * pair + 1] = both[:, FEAT:].astype(BF16)
-        return carry
-
-    lax.fori_loop(0, PEERS // 2, base_block, 0)
+
+    def base_blocks(place):
+        if place == 0:
+            loads[0].wait()
+            loads[1].wait()
+        half = PEERS // 4
+        lax.fori_loop(place * half, place * half + half, lambda pair, carry: (base_block(pair), carry)[1], 0)
 
     def base_copy(index):
         offset = OFFSETS[index]
@@ -161,26 +170,38 @@
             part_out.at[other_x * YS + other_y], part_in.at[index], base_send.at[index], base_recv.at[index], peer_id(offset)
         )
 
-    for index in range(len(OFFSETS)):
-        base_copy(index).start()
-    base[...] = jnp.dot(
-        act[...], kv[:, pl.ds(pl.multiple_of(tensor * FEAT, FEAT), FEAT)], preferred_element_type=F32
-    )
-
-    for copy in loads[2:]:
-        copy.wait()
-    sib_copy(0, 0, core).start()
-    slot_row = slots[...]
-    named = jnp.zeros((1, REQ), jnp.int32)
-    for slot in range(SLOTS):
-        named = jnp.where(slot_row == slot, owners[slot] * HELD + locals_[slot], named)
-    adapter[...] = jnp.broadcast_to(named, adapter.shape)
-    act_t[...] = act[...].T
-    slot_column = jnp.broadcast_to(slot_row, (FEAT, REQ)).T
-    lane_slot = lax.broadcasted_iota(jnp.int32, (REQ, FEAT), 1) // RANK
-    for pair in range(SLOTS // 2):
-        hot[:, pair * FEAT : (pair + 1) * FEAT] = jnp.where(slot_column == lane_slot + 2 * pair, 1.0, 0.0).astype(BF16)
-    picked[...] = jnp.zeros_like(picked)
+    def own_base():
+        base[...] = jnp.dot(
+            act[...], kv[:, pl.ds(pl.multiple_of(tensor * FEAT, FEAT), FEAT)], preferred_element_type=F32
+        )
+
+    def adapters():
+        for copy in loads[2:]:
+            copy.wait()
+        slot_row = slots[...]
+        named = jnp.zeros((1, REQ), jnp.int32)
+        for slot in range(SLOTS):
+            named = jnp.where(slot_row == slot, owners[slot] * HELD + locals_[slot], named)
+        adapter[...] = jnp.broadcast_to(named, adapter.shape)
+        act_t[...] = act[...].T
+        picked[...] = jnp.zeros_like(picked)
+
+    def hot_slots(place):
+        slot_column = jnp.broadcast_to(slots[...], (FEAT, REQ)).T
+        lane_slot = lax.broadcasted_iota(jnp.int32, (REQ, FEAT), 1) // RANK
+        for pair in range(4 * place, 4 * place + 4):
+            hot[:, pair * FEAT : (pair + 1) * FEAT] = jnp.where(slot_column == lane_slot + 2 * pair, 1.0, 0.0).astype(BF16)
+
+    def first_work(place):
+        if place < 2:
+            base_blocks(place)
+        elif place == 2:
+            for index in range(len(OFFSETS)):
+                base_copy(index).start()
+            own_base()
+        else:
+            adapters()
+            sib_copy(0, 0, core).start()
 
     def shrink_with(owner, first=0, count=HELD):
         weights = shrinks[owner, pl.ds(first, count)].reshape(count * RANK, WIDTH)
@@ -203,13 +224,26 @@
             sib_copy(0, hop, 1 - core).wait_recv()
             shrink_with(owner_at(0, hop, 1 - core))
         else:
-            @pl.when(hop > 0)
-            def _():
-                sib_copy(1, hop, 1 - core).wait_recv()
-
+            sib_copy(1, hop, 1 - core).wait_recv()
             shrink_with(owner_at(1, hop, 1 - core))
 
-    def shrink_hop(hop, carry):
+    def own_work(place):
+        if place == 0:
+            shrink_with(dp)
+        elif place == 1:
+            sib_copy(0, 0, 1 - core).wait_recv()
+            shrink_with(sibling["dp"])
+
+    def early(place, hop):
+        pl.when(hop == 1)(functools.partial(first_work, place))
+        pl.when(hop == 2)(functools.partial(own_work, place))
+        pl.when(hop == 3)(functools.partial(hot_slots, place))
+        pl.when(hop > 1)(functools.partial(work, place, hop - 1))
+
+    def late(place, hop):
+        work(place, hop - 1)
+
+    def shrink_hop(extra, hop, carry):
         for place in range(HELD):
             for way in (0, 1):
                 chunk = ORDERS[way][place]
@@ -218,17 +252,17 @@
                     ring_forward(way, hop, chunk)
                 else:
                     pl.when(hop < HALF - 1)(functools.partial(ring_forward, way, hop, chunk))
-            work(place, hop - 1)
+            extra(place, hop)
         for way in (0, 1):
             sib_copy(way, hop, core).start()
         return carry
 
-    lax.fori_loop(1, 5, shrink_hop, 0)
+    lax.fori_loop(1, 5, functools.partial(shrink_hop, early), 0)
     up_forward(0, 0)
     up_forward(1, 0)
     upsib_copy(0, 0, core).start()
     for hop in range(5, HALF):
-        shrink_hop(hop, 0)
+        shrink_hop(late, hop, 0)
         up_hop(hop - 4)
         for index in range(5 * (hop - 5), 5 * (hop - 4)):
             add_base(index)
@@ -263,8 +297,7 @@
 
     for index in range(len(OFFSETS)):
         sum_copy(index).start()
-    up_hop(6)
-    up_hop(5)
+    up_arrived(6, 0)
     total = piece_of(picked, x, y)[...]
     for index in reversed(range(len(OFFSETS))):
         sum_copy(index).wait_recv()
@@ -272,13 +305,35 @@
     piece_of(shrunk_t, x, y)[...] = total.astype(BF16)
     for index in range(len(OFFSETS)):
         all_copy(index).start()
+    up_arrived(6, 1)
+    up_shared(6)
+    up_hop(5)
+    for index in range(len(OFFSETS)):
+        base_copy(index).wait_send()
+        sum_copy(index).wait_send()
+    for way in (0, 1):
+        for hop in range(HALF):
+            for chunk in range(HELD):
+                if hop < HALF - 1 or chunk in KEPT[way]:
+                    ring_copy(way, hop, chunk, shrinks.at[owner_at(way, hop), chunk]).wait_send()
+            for piece in (0, 1):
+                if hop < 6:
+                    for copy in up_sends(way, hop, piece):
+                        copy.wait_send()
+        for hop in range(HALF + 1):
+            if hop or way == 0:
+                (sib_half(way, core) if hop == HALF else sib_copy(way, hop, core)).wait_send()
+                if hop < 5:
+                    upsib_copy(way, hop, core).wait_send()
+    up_hop(7)
+    up_hop(HALF)
     for index in reversed(range(len(OFFSETS))):
         all_copy(index, -1).wait_recv()
+    for index in range(len(OFFSETS)):
+        all_copy(index).wait_send()
     twice = jnp.concatenate([shrunk_t[...], shrunk_t[...]], axis=0).T
     for pair in range(SLOTS // 2):
         hot[:, pair * FEAT : (pair + 1) * FEAT] *= twice
-    up_hop(7)
-    up_hop(HALF)
     upsib_copy(0, 0, 1 - core).wait_recv()
     for hop in range(1, HALF + 1):
         for way in (0, 1):
@@ -288,21 +343,11 @@
     out[...] = (base[...] + jnp.dot(hot[...], rows[...], preferred_element_type=F32)).astype(BF16)
 
     for way in (0, 1):
-        for hop in range(HALF):
-            for chunk in range(HELD):
-                if hop < HALF - 1 or chunk in KEPT[way]:
-                    ring_copy(way, hop, chunk, shrinks.at[owner_at(way, hop), chunk]).wait_send()
-            for piece in (0, 1):
-                for copy in up_sends(way, hop, piece):
-                    copy.wait_send()
-        for hop in range(HALF + 1):
-            if hop or way == 0:
-                (sib_half(way, core) if hop == HALF else sib_copy(way, hop, core)).wait_send()
-                upsib_copy(way, hop, core).wait_send()
-    for index in range(len(OFFSETS)):
-        base_copy(index).wait_send()
-        sum_copy(index).wait_send()
-        all_copy(index).wait_send()
+        for piece in (0, 1):
+            for copy in up_sends(way, 6, piece):
+                copy.wait_send()
+        for hop in range(5, HALF + 1):
+            upsib_copy(way, hop, core).wait_send()
 
 
 def shards(activations, kv_weight, pool_shrink, pool_expand, request_slot, slot_owner, slot_local):

time: 84.4 us -> 81.9 us (0.970)
  Pallas kernels: 82.7 us -> 80.2 us
    pallas_call x1, Pallas kernels: 82.7 us -> 80.2 us  [shards(): pl.pallas_call(kernel, out_shape=jax.ShapeDtypeStruct((REQ, FEAT), BF16),...]
where the time goes in v3:
time: 81.9 us; the launch traced here: 81.8 us
  Pallas kernels  80.2 us (98%)
  local copies, waits for them, and re-layouts  1.57 us (2%)
    pallas_call x1, Pallas kernels, shards(): pl.pallas_call(kernel, out_shape=jax.ShapeDtypeStruct((REQ, FEAT), BF16),...  80.2 us

profile of v3, /device:TPU:1, one launch (start us, length us, event | category | flops | bytes accessed | tf_op | source)
XLA Modules:
  0.0 81.8 jit_solution(7332328906107398221)
XLA Ops:
  0.0 80.2 %shard_map.73 = bf16[512,128]{1,0:T(8,128)(2,1)} custom-call(s32[32]{0:T(128)} %bitcast.4, s32[32]{0:T(128)} %bitcast.5, s32[1,512]{1,0:T(1,128)} %bitcast.3, bf16[512,512]{1,0:T(8,128)(2,1)} %act_hbm.1, bf16[512,2048]{1,0:T(8,128)(2,1)} %kv_hbm.1, bf16[4,64,512]{2,1,0:T(8,128)(2,1)} %shrink_hbm.1, bf16[4,64,128]{2,1,0:T(8,128)(2,1)} %expand_hbm.1), custom_call_target="tpu_custom_call" | custom-call | tf_op jit(solution)/shard_map/pallas_call | solution.py:358
  80.2 1.6 %copy.9 = bf16[512,128]{1,0:T(8,128)(2,1)} copy(bf16[512,128]{1,0:T(8,128)(2,1)} %shard_map.73) | data formatting | bytes 262144

commit v4 on v3

--- a/solution.py
+++ b/solution.py
@@ -49,6 +49,11 @@
     next_of = ({"dp": owner_at(1, 1)}, {"dp": owner_at(0, 1)})
     after_next = ({"dp": owner_at(1, 2)}, {"dp": owner_at(0, 2)})
     sibling = {"dp": z * CORES + 1 - core}
+
+    def in_bytes(ref, semaphore):
+        return remote(ref, ref, semaphore, semaphore, sibling)
+
+    all_pieces = rows.at[pl.ds(0, 16 * len(OFFSETS))]
 
     def peer(offset, sign=1):
         other_x = (x + sign * offset[0] + XS) % XS
@@ -79,7 +84,7 @@
 
     def ring_copy(way, hop, chunk, src):
         return remote(
-            src, shrinks.at[owner_at(way, hop), chunk], ring_send.at[way, hop, chunk],
+            src, shrinks.at[owner_at(way, hop), chunk], ring_send.at[0],
             ring_recv.at[way, hop, chunk], next_of[way],
         )
 
@@ -89,17 +94,17 @@
     def ring_arrived(way, hop, chunk):
         owner = owner_at(way, hop)
         remote(
-            shrinks.at[owner, chunk], shrinks.at[owner, chunk], ring_send.at[way, hop, chunk],
+            shrinks.at[owner, chunk], shrinks.at[owner, chunk], ring_send.at[0],
             ring_recv.at[way, hop - 1, chunk], next_of[way],
         ).wait_recv()
 
     def sib_copy(way, hop, which):
         shard = shrinks.at[owner_at(way, hop, which)]
-        return remote(shard, shard, sib_send.at[way, hop], sib_recv.at[way, hop], sibling)
+        return remote(shard, shard, sib_send.at[0], sib_recv.at[way, hop], sibling)
 
     def sib_half(way, which):
         shard = shrinks.at[owner_at(way, HALF, which), pl.ds(2 * way, 2)]
-        return remote(shard, shard, sib_send.at[way, HALF], sib_recv.at[way, HALF], sibling)
+        return remote(shard, shard, sib_send.at[0], sib_recv.at[way, HALF], sibling)
 
     def up_part(way, hop):
         return pl.ds(2 * way, 2) if hop == HALF else pl.ds(0, HELD)
@@ -107,7 +112,7 @@
     def up_copy(way, hop, owner, piece, step=1):
         part = expands.at[owner, pl.ds(2 * piece, 2)]
         device = next_of[way] if step == 1 else after_next[way]
-        return remote(part, part, up_send.at[way, hop, piece, step - 1], up_recv.at[way, hop + step - 1, piece], device)
+        return remote(part, part, up_send.at[0], up_recv.at[way, hop + step - 1, piece], device)
 
     def up_sends(way, hop, piece):
         if hop < EXPAND_LATE:
@@ -127,7 +132,7 @@
 
     def upsib_copy(way, hop, which):
         shard = expands.at[owner_at(way, hop, which), up_part(way, hop)]
-        return remote(shard, shard, upsib_send.at[way, hop], upsib_recv.at[way, hop], sibling)
+        return remote(shard, shard, upsib_send.at[0], upsib_recv.at[0], sibling)
 
     def up_arrived(hop, turn):
         for way in (0, 1):
@@ -167,7 +172,7 @@
         offset = OFFSETS[index]
         other_x, other_y = peer(offset)
         return remote(
-            part_out.at[other_x * YS + other_y], part_in.at[index], base_send.at[index], base_recv.at[index], peer_id(offset)
+            part_out.at[other_x * YS + other_y], part_in.at[index], base_send.at[0], base_recv.at[index // 5], peer_id(offset)
         )
 
     def own_base():
@@ -213,7 +218,8 @@
         picked[...] = total
 
     def add_base(index):
-        base_copy(index).wait_recv()
+        if index % 5 == 0:
+            in_bytes(part_in.at[pl.ds(index, 5)], base_recv.at[index // 5]).wait_recv()
         base[...] += part_in[index].astype(F32)
 
     def work(place, hop):
@@ -285,13 +291,12 @@
     def sum_copy(index):
         other_x, other_y = peer(OFFSETS[index])
         return remote(
-            piece_of(picked, other_x, other_y), sum_in.at[index], sum_send.at[index], sum_recv.at[index], peer_id(OFFSETS[index])
+            piece_of(picked, other_x, other_y), sum_in.at[index], sum_send.at[0], sum_recv.at[0], peer_id(OFFSETS[index])
         )
 
-    def all_copy(index, sign=1):
-        at_x, at_y = (x, y) if sign == 1 else peer(OFFSETS[index], -1)
+    def all_copy(index):
         return remote(
-            piece_of(shrunk_t, at_x, at_y), piece_of(shrunk_t, at_x, at_y), all_send.at[index], all_recv.at[index],
+            piece_of(shrunk_t, x, y), piece_of(shrunk_t, x, y), all_send.at[0], all_recv.at[0],
             peer_id(OFFSETS[index]),
         )
 
@@ -299,8 +304,8 @@
         sum_copy(index).start()
     up_arrived(6, 0)
     total = piece_of(picked, x, y)[...]
-    for index in reversed(range(len(OFFSETS))):
-        sum_copy(index).wait_recv()
+    in_bytes(sum_in, sum_recv.at[0]).wait_recv()
+    for index in range(len(OFFSETS)):
         total += sum_in[index]
     piece_of(shrunk_t, x, y)[...] = total.astype(BF16)
     for index in range(len(OFFSETS)):
@@ -308,46 +313,25 @@
     up_arrived(6, 1)
     up_shared(6)
     up_hop(5)
-    for index in range(len(OFFSETS)):
-        base_copy(index).wait_send()
-        sum_copy(index).wait_send()
-    for way in (0, 1):
-        for hop in range(HALF):
-            for chunk in range(HELD):
-                if hop < HALF - 1 or chunk in KEPT[way]:
-                    ring_copy(way, hop, chunk, shrinks.at[owner_at(way, hop), chunk]).wait_send()
-            for piece in (0, 1):
-                if hop < 6:
-                    for copy in up_sends(way, hop, piece):
-                        copy.wait_send()
-        for hop in range(HALF + 1):
-            if hop or way == 0:
-                (sib_half(way, core) if hop == HALF else sib_copy(way, hop, core)).wait_send()
-                if hop < 5:
-                    upsib_copy(way, hop, core).wait_send()
     up_hop(7)
     up_hop(HALF)
-    for index in reversed(range(len(OFFSETS))):
-        all_copy(index, -1).wait_recv()
-    for index in range(len(OFFSETS)):
-        all_copy(index).wait_send()
+    in_bytes(all_pieces, all_recv.at[0]).wait_recv()
     twice = jnp.concatenate([shrunk_t[...], shrunk_t[...]], axis=0).T
     for pair in range(SLOTS // 2):
         hot[:, pair * FEAT : (pair + 1) * FEAT] *= twice
-    upsib_copy(0, 0, 1 - core).wait_recv()
-    for hop in range(1, HALF + 1):
-        for way in (0, 1):
-            upsib_copy(way, hop, 1 - core).wait_recv()
+    in_bytes(expands.at[pl.ds(0, PLANES)], upsib_recv.at[0]).wait_recv()
     for slot in range(SLOTS):
         rows[slot * RANK : (slot + 1) * RANK, :] = expands[owners[slot], locals_[slot]]
     out[...] = (base[...] + jnp.dot(hot[...], rows[...], preferred_element_type=F32)).astype(BF16)
 
-    for way in (0, 1):
-        for piece in (0, 1):
-            for copy in up_sends(way, 6, piece):
-                copy.wait_send()
-        for hop in range(5, HALF + 1):
-            upsib_copy(way, hop, core).wait_send()
+    chunks = 2 * ((HALF - 1) * HELD + 2)
+    in_bytes(shrinks.at[pl.ds(0, chunks // HELD)], ring_send.at[0]).wait_send()
+    in_bytes(shrinks.at[pl.ds(0, PLANES)], sib_send.at[0]).wait_send()
+    in_bytes(expands.at[pl.ds(0, PLANES - 1)], up_send.at[0]).wait_send()
+    in_bytes(expands.at[pl.ds(0, PLANES)], upsib_send.at[0]).wait_send()
+    in_bytes(part_in, base_send.at[0]).wait_send()
+    in_bytes(sum_in, sum_send.at[0]).wait_send()
+    in_bytes(all_pieces, all_send.at[0]).wait_send()
 
 
 def shards(activations, kv_weight, pool_shrink, pool_expand, request_slot, slot_owner, slot_local):
@@ -379,20 +363,20 @@
             pltpu.VMEM((REQ, SLOTS * RANK), BF16),
             pltpu.VMEM((SLOTS * RANK, FEAT), BF16),
             dma((7,)),
+            dma((1,)),
             dma((2, HALF, HELD)),
-            dma((2, HALF, HELD)),
+            dma((1,)),
             dma((2, HALF + 1)),
-            dma((2, HALF + 1)),
-            dma((2, HALF, 2, 2)),
+            dma((1,)),
             dma((2, HALF, 2)),
-            dma((2, HALF + 1)),
-            dma((2, HALF + 1)),
-            dma((peers,)),
-            dma((peers,)),
-            dma((peers,)),
-            dma((peers,)),
-            dma((peers,)),
-            dma((peers,)),
+            dma((1,)),
+            dma((1,)),
+            dma((1,)),
+            dma((3,)),
+            dma((1,)),
+            dma((1,)),
+            dma((1,)),
+            dma((1,)),
         ],
         compiler_params=pltpu.CompilerParams(
             collective_id=0, has_side_effects=True, vmem_limit_bytes=60 * 2**20

time: 81.9 us -> 79.6 us (0.972)
  Pallas kernels: 80.2 us -> 77.9 us
    pallas_call x1, Pallas kernels: 80.2 us -> 77.9 us  [shards(): pl.pallas_call(kernel, out_shape=jax.ShapeDtypeStruct((REQ, FEAT), BF16),...]
where the time goes in v4:
time: 79.6 us; the launch traced here: 79.5 us
  Pallas kernels  77.9 us (98%)
  local copies, waits for them, and re-layouts  1.57 us (2%)
    pallas_call x1, Pallas kernels, shards(): pl.pallas_call(kernel, out_shape=jax.ShapeDtypeStruct((REQ, FEAT), BF16),...  77.9 us

profile of v4, /device:TPU:1, one launch (start us, length us, event | category | flops | bytes accessed | tf_op | source)
XLA Modules:
  0.0 79.5 jit_solution(17311200026441652027)
XLA Ops:
  0.0 77.9 %shard_map.73 = bf16[512,128]{1,0:T(8,128)(2,1)} custom-call(s32[32]{0:T(128)} %bitcast.4, s32[32]{0:T(128)} %bitcast.5, s32[1,512]{1,0:T(1,128)} %bitcast.3, bf16[512,512]{1,0:T(8,128)(2,1)} %act_hbm.1, bf16[512,2048]{1,0:T(8,128)(2,1)} %kv_hbm.1, bf16[4,64,512]{2,1,0:T(8,128)(2,1)} %shrink_hbm.1, bf16[4,64,128]{2,1,0:T(8,128)(2,1)} %expand_hbm.1), custom_call_target="tpu_custom_call" | custom-call | tf_op jit(solution)/shard_map/pallas_call | solution.py:342
  77.9 1.6 %copy.9 = bf16[512,128]{1,0:T(8,128)(2,1)} copy(bf16[512,128]{1,0:T(8,128)(2,1)} %shard_map.73) | data formatting | bytes 262144

commit v5 on v4

--- a/solution.py
+++ b/solution.py
@@ -14,8 +14,6 @@
 HELD, RANK, SLOTS = 4, 64, 32
 REQ, WIDTH, FEAT = 512, 512, 128
 HALF = PLANES // 2
-ORDERS = ((0, 1, 2, 3), (2, 3, 0, 1))
-KEPT = ((0, 1), (2, 3))
 EXPAND_LATE = 4
 
 
@@ -82,21 +80,18 @@
         copy.start()
     pl.semaphore_wait(barrier, 5 + len(OFFSETS))
 
-    def ring_copy(way, hop, chunk, src):
+    def ring_copy(way, hop, piece, src):
         return remote(
-            src, shrinks.at[owner_at(way, hop), chunk], ring_send.at[0],
-            ring_recv.at[way, hop, chunk], next_of[way],
-        )
-
-    def ring_forward(way, hop, chunk):
-        ring_copy(way, hop, chunk, shrinks.at[owner_at(way, hop), chunk]).start()
-
-    def ring_arrived(way, hop, chunk):
-        owner = owner_at(way, hop)
-        remote(
-            shrinks.at[owner, chunk], shrinks.at[owner, chunk], ring_send.at[0],
-            ring_recv.at[way, hop - 1, chunk], next_of[way],
-        ).wait_recv()
+            src, shrinks.at[owner_at(way, hop), pl.ds(2 * piece, 2)], ring_send.at[0],
+            ring_recv.at[way, hop, piece], next_of[way],
+        )
+
+    def ring_forward(way, hop, piece):
+        ring_copy(way, hop, piece, shrinks.at[owner_at(way, hop), pl.ds(2 * piece, 2)]).start()
+
+    def ring_arrived(way, hop, piece):
+        part = shrinks.at[owner_at(way, hop), pl.ds(2 * piece, 2)]
+        remote(part, part, ring_send.at[0], ring_recv.at[way, hop - 1, piece], next_of[way]).wait_recv()
 
     def sib_copy(way, hop, which):
         shard = shrinks.at[owner_at(way, hop, which)]
@@ -151,10 +146,10 @@
             up_arrived(hop, turn)
         up_shared(hop)
 
-    for place in range(HELD):
+    for turn in (0, 1):
         for way in (0, 1):
-            chunk = ORDERS[way][place]
-            ring_copy(way, 0, chunk, shrink_hbm.at[chunk]).start()
+            piece = way if turn == 0 else 1 - way
+            ring_copy(way, 0, piece, shrink_hbm.at[pl.ds(2 * piece, 2)]).start()
 
     def base_block(pair):
         both = jnp.dot(act[...], kv[:, pl.ds(pl.multiple_of(pair * 2 * FEAT, 2 * FEAT), 2 * FEAT)], preferred_element_type=F32)
@@ -250,15 +245,16 @@
         work(place, hop - 1)
 
     def shrink_hop(extra, hop, carry):
-        for place in range(HELD):
+        for turn in (0, 1):
             for way in (0, 1):
-                chunk = ORDERS[way][place]
-                ring_arrived(way, hop, chunk)
-                if chunk in KEPT[way]:
-                    ring_forward(way, hop, chunk)
+                piece = way if turn == 0 else 1 - way
+                ring_arrived(way, hop, piece)
+                if turn == 0:
+                    ring_forward(way, hop, piece)
                 else:
-                    pl.when(hop < HALF - 1)(functools.partial(ring_forward, way, hop, chunk))
-            extra(place, hop)
+                    pl.when(hop < HALF - 1)(functools.partial(ring_forward, way, hop, piece))
+            extra(2 * turn, hop)
+            extra(2 * turn + 1, hop)
         for way in (0, 1):
             sib_copy(way, hop, core).start()
         return carry
@@ -275,8 +271,7 @@
     for place in range(HELD):
         work(place, HALF - 1)
     for way in (0, 1):
-        for place in (0, 1):
-            ring_arrived(way, HALF, ORDERS[way][place])
+        ring_arrived(way, HALF, way)
         sib_half(way, core).start()
     up_hop(EXPAND_LATE)
     for way in (0, 1):
@@ -364,7 +359,7 @@
             pltpu.VMEM((SLOTS * RANK, FEAT), BF16),
             dma((7,)),
             dma((1,)),
-            dma((2, HALF, HELD)),
+            dma((2, HALF, 2)),
             dma((1,)),
             dma((2, HALF + 1)),
             dma((1,)),

time: 79.6 us -> 80 us (level)
  no operation moved by 1% of the time
where the time goes in v5:
time: 80 us; the launch traced here: 79.8 us
  Pallas kernels  78.3 us (98%)
  local copies, waits for them, and re-layouts  1.57 us (2%)
    pallas_call x1, Pallas kernels, shards(): pl.pallas_call(kernel, out_shape=jax.ShapeDtypeStruct((REQ, FEAT), BF16),...  78.3 us

profile of v5, /device:TPU:1, one launch (start us, length us, event | category | flops | bytes accessed | tf_op | source)
XLA Modules:
  0.0 79.8 jit_solution(7709367745375173135)
XLA Ops:
  0.0 78.3 %shard_map.73 = bf16[512,128]{1,0:T(8,128)(2,1)} custom-call(s32[32]{0:T(128)} %bitcast.4, s32[32]{0:T(128)} %bitcast.5, s32[1,512]{1,0:T(1,128)} %bitcast.3, bf16[512,512]{1,0:T(8,128)(2,1)} %act_hbm.1, bf16[512,2048]{1,0:T(8,128)(2,1)} %kv_hbm.1, bf16[4,64,512]{2,1,0:T(8,128)(2,1)} %shrink_hbm.1, bf16[4,64,128]{2,1,0:T(8,128)(2,1)} %expand_hbm.1), custom_call_target="tpu_custom_call" | custom-call | tf_op jit(solution)/shard_map/pallas_call | solution.py:337
  78.3 1.6 %copy.9 = bf16[512,128]{1,0:T(8,128)(2,1)} copy(bf16[512,128]{1,0:T(8,128)(2,1)} %shard_map.73) | data formatting | bytes 262144
